TPU v7x, 32 devices: a whole 2x2x4 slice. The times are simulated.
32 devices in a mesh: row: 4 (over x, core), col: 8 (over z, y).
Axes of the slice: x: 2, y: 2, z: 4, core: 2. Of those that a mesh axis runs over, the one named last changes fastest.
Arguments:
- slab_feat: bfloat16 [8192, 64], P(('row', 'col')), may hold values from -0.8984375 to 0.8984375
- slab_left: bfloat16 [8192, 32], P(('row', 'col')), may hold values from -6 to 6
- points: bfloat16 [16384, 64], P('col'), may hold values from -0.8984375 to 0.8984375
- right_vec: bfloat16 [16384, 32], P('col'), may hold values from -6 to 6
- inv_length: float32 [64], replicated, may hold values from 0.5 to 2
Outputs:
- slab_grad: float32 [8192, 64], P(('row', 'col'))
- point_grad: float32 [16384, 64], P('col')
All inputs are finite; a program needn't handle non-finite values.
Results may differ from a plain program's by a relative error of at most 0.0075.
Values may be sent and summed in bfloat16 or wider, within the bound.
A program may use at most 64 MiB of HBM per device.

v0:
```python
import math

import jax
import jax.numpy as jnp
from jax import lax
from jax.sharding import PartitionSpec as P


def sweep(xs, left, zs, right, inv_length):
    rows, width = xs.shape
    cols = zs.shape[0]
    ranks = left.shape[1]
    row_block = min(2048, rows)
    col_block = min(256, cols)
    sq_x = jnp.sum(jnp.square(xs.astype(jnp.float32)), 1)
    sq_z = jnp.sum(jnp.square(zs.astype(jnp.float32)), 1)
    zs_blocks = zs.reshape(cols // col_block, col_block, width)
    right_blocks = right.reshape(cols // col_block, col_block, ranks)
    sqz_blocks = sq_z.reshape(cols // col_block, col_block)
    xs_blocks = xs.reshape(rows // row_block, row_block, width)
    left_blocks = left.reshape(rows // row_block, row_block, ranks)
    sqx_blocks = sq_x.reshape(rows // row_block, row_block)

    def row_step(carry, pieces):
        trans_acc, col_mass = carry
        x_blk, l_blk, sx_blk = pieces

        def col_step(inner, cpieces):
            gz_acc, mass = inner
            z_blk, r_blk, sz_blk = cpieces
            cross = jnp.einsum("ik,jk->ij", x_blk, z_blk, preferred_element_type=jnp.float32)
            kern = jnp.exp(-0.5 * (sx_blk[:, None] + sz_blk[None, :] - 2.0 * cross))
            weight = jnp.einsum("ik,jk->ij", l_blk, r_blk, preferred_element_type=jnp.float32)
            prod = weight * kern
            prod_b = prod.astype(jnp.bfloat16)
            gz_acc = gz_acc + jnp.dot(prod_b, z_blk, preferred_element_type=jnp.float32)
            mass = mass + jnp.sum(prod, 1)
            trans = jnp.einsum("ij,ik->jk", prod_b, x_blk, preferred_element_type=jnp.float32)
            return ((gz_acc, mass), (trans, jnp.sum(prod, 0)))

        start = (jnp.zeros((row_block, width), jnp.float32), jnp.zeros((row_block,), jnp.float32))
        (gz_acc, mass), (trans, cmass) = lax.scan(
            col_step, start, (zs_blocks, right_blocks, sqz_blocks)
        )
        trans_acc = trans_acc + trans.reshape(cols, width)
        col_mass = col_mass + cmass.reshape(cols)
        row_term = gz_acc - mass[:, None] * x_blk.astype(jnp.float32)
        return ((trans_acc, col_mass), row_term)

    init = (jnp.zeros((cols, width), jnp.float32), jnp.zeros((cols,), jnp.float32))
    (trans_acc, col_mass), row_terms = lax.scan(
        row_step, init, (xs_blocks, left_blocks, sqx_blocks)
    )
    row_term = row_terms.reshape(rows, width) * inv_length[None, :]
    col_term = (trans_acc - col_mass[:, None] * zs.astype(jnp.float32)) * inv_length[None, :]
    return (row_term, col_term)


def local(slab_feat, slab_left, points, right_vec, inv_length):
    ranks = slab_left.shape[1]
    total = points.shape[0] * lax.axis_size("col")
    coef = jnp.where(jnp.arange(ranks) == 0, 0.5, -0.5 / (ranks - 1)).astype(jnp.float32)
    xs = (slab_feat.astype(jnp.float32) * inv_length[None, :]).astype(jnp.bfloat16)
    zs = (points.astype(jnp.float32) * inv_length[None, :]).astype(jnp.bfloat16)
    left = (slab_left.astype(jnp.float32) * coef[None, :] * (64.0 / math.sqrt(total))).astype(
        jnp.bfloat16
    )
    xs_group, left_group = (
        lax.all_gather(xs, "col", axis=0, tiled=True),
        lax.all_gather(left, "col", axis=0, tiled=True),
    )
    row_term, col_term = sweep(xs_group, left_group, zs, right_vec, inv_length)
    slab_grad = lax.psum_scatter(row_term, "col", scatter_dimension=0, tiled=True)
    point_grad = lax.psum(col_term, "row")
    return (slab_grad, point_grad)


def solution(mesh):
    placed = (P(("row", "col"), None), P(("row", "col"), None), P("col", None), P("col", None), P())
    return jax.shard_map(
        local,
        mesh=mesh,
        in_specs=placed,
        out_specs=(P(("row", "col"), None), P("col", None)),
        check_vma=False,
    )
```

profile of v0, /device:TPU:1, one launch (start us, length us, event | category | flops | bytes accessed | tf_op | source)
XLA Modules:
  0.0 209.4 jit_solution(14713276299498965951)
XLA Ops:
  8.1 0.9 multiply_convert_fusion.1
  8.9 25.9 %all_gather.7 = bf16[2048,64]{0,1:T(8,128)(2,1)S(1)} all-gather(bf16[256,64]{0,1:T(8,128)(2,1)S(1)} %multiply_convert_fusion.1), channel_id=1, replica_groups=mesh['row'=4,'col'=8] {'col'}, dimensions={0}, use_global_device_ids=true | all-gather | bytes 294912 | tf_op jit(solution)/shard_map/all_gather | solution.py:69
  34.9 0.3 copy.15
  35.1 0.1 fusion.16
  35.3 1.1 fusion.19
  36.4 1.0 copy.17
  37.4 0.1 multiply_convert_fusion.2
  37.5 24.4 %all_gather.6 = bf16[2048,32]{0,1:T(8,128)(2,1)S(1)} all-gather(bf16[256,32]{0,1:T(8,128)(2,1)S(1)} %multiply_convert_fusion.2), channel_id=1, replica_groups=mesh['row'=4,'col'=8] {'col'}, dimensions={0}, use_global_device_ids=true | all-gather | bytes 147456 | tf_op jit(solution)/shard_map/all_gather | solution.py:70
  61.9 0.3 copy.13
  62.2 1.0 copy.12
  63.2 56.2 %while.29 = (s32[]{:T(128)}, f32[2048,64]{0,1:T(8,128)S(1)}, f32[2048]{0:T(1024)S(1)}, f32[8,256,64]{1,0,2:T(8,128)}, f32[8,256]{1,0:T(8,128)S(1)}, /*index=5*/b...) while((s32[]{:T(128)}, f32[2048,64]{0,1:T(8,128)S(1)}, ...), condition=%wide.region_5.6_spmd.clone, body=%wide.region_2.5_spmd.clone.sunk | while | flops 239339264 | bytes 9617044 | solution.py:42
  63.2 1.4 fusion.44
  64.6 1.4 fusion.45
  66.0 0.5 convolution_bitcast_fusion.3
  66.5 0.1 copy.25
  66.6 2.4 %dynamic_update_slice.15 = f32[8,256,64]{1,0,2:T(8,128)} dynamic-update-slice(f32[8,256,64]{1,0,2:T(8,128)} %get-tuple-element.275, f32[1,256,64]{1,0,2:T(1,128)S(1)} %copy.25, s32[]{:T(128)} %get-tuple-element.272, s32[]{:T(128)} %constant.21.clone.1..sunk, s32[]{:T(128)} %constant.21.clone.1..sunk) | dynamic-update-slice | bytes 131076 | tf_op jit(solution)/shard_map/while/body/eval_jaxpr/while/body/jit(dynamic_update_index_in_dim)/dynamic_update_slice | solution.py:42
  69.0 1.2 convolution_add_fusion.2
  70.2 1.4 fusion.44
  71.7 1.4 fusion.45
  73.1 0.5 convolution_bitcast_fusion.3
  73.5 0.1 copy.25
  73.6 2.4 %dynamic_update_slice.15 = f32[8,256,64]{1,0,2:T(8,128)} dynamic-update-slice(f32[8,256,64]{1,0,2:T(8,128)} %get-tuple-element.275, f32[1,256,64]{1,0,2:T(1,128)S(1)} %copy.25, s32[]{:T(128)} %get-tuple-element.272, s32[]{:T(128)} %constant.21.clone.1..sunk, s32[]{:T(128)} %constant.21.clone.1..sunk) | dynamic-update-slice | bytes 131076 | tf_op jit(solution)/shard_map/while/body/eval_jaxpr/while/body/jit(dynamic_update_index_in_dim)/dynamic_update_slice | solution.py:42
  76.0 1.2 convolution_add_fusion.2
  77.3 1.4 fusion.44
  78.7 1.4 fusion.45
  80.1 0.5 convolution_bitcast_fusion.3
  80.6 0.1 copy.25
  80.6 2.4 %dynamic_update_slice.15 = f32[8,256,64]{1,0,2:T(8,128)} dynamic-update-slice(f32[8,256,64]{1,0,2:T(8,128)} %get-tuple-element.275, f32[1,256,64]{1,0,2:T(1,128)S(1)} %copy.25, s32[]{:T(128)} %get-tuple-element.272, s32[]{:T(128)} %constant.21.clone.1..sunk, s32[]{:T(128)} %constant.21.clone.1..sunk) | dynamic-update-slice | bytes 131076 | tf_op jit(solution)/shard_map/while/body/eval_jaxpr/while/body/jit(dynamic_update_index_in_dim)/dynamic_update_slice | solution.py:42
  83.0 1.2 convolution_add_fusion.2
  84.3 1.4 fusion.44
  85.7 1.4 fusion.45
  87.1 0.5 convolution_bitcast_fusion.3
  87.6 0.1 copy.25
  87.7 2.4 %dynamic_update_slice.15 = f32[8,256,64]{1,0,2:T(8,128)} dynamic-update-slice(f32[8,256,64]{1,0,2:T(8,128)} %get-tuple-element.275, f32[1,256,64]{1,0,2:T(1,128)S(1)} %copy.25, s32[]{:T(128)} %get-tuple-element.272, s32[]{:T(128)} %constant.21.clone.1..sunk, s32[]{:T(128)} %constant.21.clone.1..sunk) | dynamic-update-slice | bytes 131076 | tf_op jit(solution)/shard_map/while/body/eval_jaxpr/while/body/jit(dynamic_update_index_in_dim)/dynamic_update_slice | solution.py:42
  90.0 1.2 convolution_add_fusion.2
  91.3 1.4 fusion.44
  92.8 1.4 fusion.45
  94.2 0.5 convolution_bitcast_fusion.3
  94.6 0.1 copy.25
  94.7 2.4 %dynamic_update_slice.15 = f32[8,256,64]{1,0,2:T(8,128)} dynamic-update-slice(f32[8,256,64]{1,0,2:T(8,128)} %get-tuple-element.275, f32[1,256,64]{1,0,2:T(1,128)S(1)} %copy.25, s32[]{:T(128)} %get-tuple-element.272, s32[]{:T(128)} %constant.21.clone.1..sunk, s32[]{:T(128)} %constant.21.clone.1..sunk) | dynamic-update-slice | bytes 131076 | tf_op jit(solution)/shard_map/while/body/eval_jaxpr/while/body/jit(dynamic_update_index_in_dim)/dynamic_update_slice | solution.py:42
  97.1 1.2 convolution_add_fusion.2
  98.4 1.4 fusion.44
  99.8 1.4 fusion.45
  101.2 0.5 convolution_bitcast_fusion.3
  101.6 0.1 copy.25
  101.7 2.4 %dynamic_update_slice.15 = f32[8,256,64]{1,0,2:T(8,128)} dynamic-update-slice(f32[8,256,64]{1,0,2:T(8,128)} %get-tuple-element.275, f32[1,256,64]{1,0,2:T(1,128)S(1)} %copy.25, s32[]{:T(128)} %get-tuple-element.272, s32[]{:T(128)} %constant.21.clone.1..sunk, s32[]{:T(128)} %constant.21.clone.1..sunk) | dynamic-update-slice | bytes 131076 | tf_op jit(solution)/shard_map/while/body/eval_jaxpr/while/body/jit(dynamic_update_index_in_dim)/dynamic_update_slice | solution.py:42
  104.1 1.2 convolution_add_fusion.2
  105.4 1.4 fusion.44
  106.8 1.4 fusion.45
  108.2 0.5 convolution_bitcast_fusion.3
  108.7 0.1 copy.25
  108.8 2.4 %dynamic_update_slice.15 = f32[8,256,64]{1,0,2:T(8,128)} dynamic-update-slice(f32[8,256,64]{1,0,2:T(8,128)} %get-tuple-element.275, f32[1,256,64]{1,0,2:T(1,128)S(1)} %copy.25, s32[]{:T(128)} %get-tuple-element.272, s32[]{:T(128)} %constant.21.clone.1..sunk, s32[]{:T(128)} %constant.21.clone.1..sunk) | dynamic-update-slice | bytes 131076 | tf_op jit(solution)/shard_map/while/body/eval_jaxpr/while/body/jit(dynamic_update_index_in_dim)/dynamic_update_slice | solution.py:42
  111.1 1.2 convolution_add_fusion.2
  112.4 1.4 fusion.44
  113.9 1.4 fusion.45
  115.2 0.5 convolution_bitcast_fusion.3
  115.8 2.4 %dynamic_update_slice.15 = f32[8,256,64]{1,0,2:T(8,128)} dynamic-update-slice(f32[8,256,64]{1,0,2:T(8,128)} %get-tuple-element.275, f32[1,256,64]{1,0,2:T(1,128)S(1)} %copy.25, s32[]{:T(128)} %get-tuple-element.272, s32[]{:T(128)} %constant.21.clone.1..sunk, s32[]{:T(128)} %constant.21.clone.1..sunk) | dynamic-update-slice | bytes 131076 | tf_op jit(solution)/shard_map/while/body/eval_jaxpr/while/body/jit(dynamic_update_index_in_dim)/dynamic_update_slice | solution.py:42
  118.2 1.2 convolution_add_fusion.2
  119.4 1.2 copy.22
  120.7 1.2 fusion.21
  122.0 0.5 reduce-scatter.2.cloned.1.call-update
  122.5 44.7 %all-reduce.2.cloned.1.call-done = f32[2048,64]{0,1:T(8,128)} async-done(((f32[2048,64]{0,1:T(8,128)}), f32[2048,64]{0,1:T(8,128)}) %all-reduce.2.cloned.1.call-update) | async-done | bytes 524304 | tf_op jit(solution)/shard_map/psum | solution.py:74
  167.2 32.8 %reduce-scatter.2.cloned.1.call-done = f32[256,64]{0,1:T(8,128)} async-done(((f32[2048,64]{0,1:T(8,128)}), f32[256,64]{0,1:T(8,128)}) %reduce-scatter.2.cloned.1.call-update) | async-done | bytes 65552 | tf_op jit(solution)/shard_map/reduce_scatter | solution.py:73
  200.1 1.9 copy.44
  (41 shorter events, 0.6 us)
Async XLA Ops:
  8.0 29.4 %copy-start.1 = (bf16[256,32]{0,1:T(8,128)(2,1)S(1)}, bf16[256,32]{0,1:T(8,128)(2,1)}, u32[]{:S(2)}) copy-start(bf16[256,32]{0,1:T(8,128)(2,1)} %param.8) | copy-start | bytes 49156
  8.0 54.2 %copy-start = (bf16[2048,32]{0,1:T(8,128)(2,1)S(1)}, bf16[2048,32]{0,1:T(8,128)(2,1)}, u32[]{:S(2)}) copy-start(bf16[2048,32]{0,1:T(8,128)(2,1)} %param.10) | copy-start | bytes 393220
  8.0 159.2 %all-reduce.2.cloned.1.call-start = ((), (), s32[]{:S(2)}) async-start(), calls=%async_computation.2 | async-start | bytes 1048576 | tf_op jit(solution)/shard_map/psum | solution.py:74
  63.2 57.5 %copy-start.2 = (f32[64]{0:T(128)S(1)}, f32[64]{0:T(128)}, u32[]{:S(2)}) copy-start(f32[64]{0:T(128)} %param.11) | copy-start | bytes 772
  121.9 78.1 %reduce-scatter.2.cloned.1.call-start = ((), (), s32[]{:S(2)}) async-start(), calls=%async_computation.1 | async-start | bytes 589824 | tf_op jit(solution)/shard_map/reduce_scatter | solution.py:73
Sparse Core Ops, SparseCore 0:
  122.0 45.1 all-reduce.1
Sparse Core Ops, SparseCore 1:
  126.3 73.7 reduce-scatter.1
where the time goes:
time: 213 us; the launch traced here: 209 us
  waiting for transfers between devices  78.1 us (37%)
  blocking collectives  50.3 us (24%)
  matrix products  35.7 us (17%)
  local copies, waits for them, and re-layouts  25.7 us (12%)
  between operations  15.6 us (7%)
  other arithmetic  3.41 us (2%)
    psum x1, waiting for transfers between devices, local(): point_grad = lax.psum(col_term, 'row')  44.7 us
    reduce_scatter x1, waiting for transfers between devices, local(): lax.psum_scatter(row_term, 'col', scatter_dimension=0, tiled=True)  32.8 us
    all_gather x1, blocking collectives, local(): lax.all_gather(xs, 'col', axis=0, tiled=True)  25.9 us
    all_gather x1, blocking collectives, local(): lax.all_gather(left, 'col', axis=0, tiled=True)  24.4 us
    dynamic_update_slice x24, local copies, waits for them, and re-layouts, row_step(): lax.scan(col_step, start, (zs_blocks, right_blocks, sqz_blocks))  20 us
    dot_general x8, matrix products, col_step(): jnp.einsum('ik,jk->ij', x_blk, z_blk, preferred_element_type=jnp.float32)  11.4 us
    dot_general x8, matrix products, col_step(): jnp.einsum('ik,jk->ij', l_blk, r_blk, preferred_element_type=jnp.float32)  11 us
    dot_general x8, matrix products, col_step(): gz_acc = gz_acc + jnp.dot(prod_b, z_blk, preferred_element_type=jnp.float32)  9.55 us
  transfers between devices with their start and end apart: 2, of which 2 were waited for; matrix products, arithmetic and copies ran while one was open for 0% of the time, Pallas kernels for 0%

commit v1 on v0

v1 whole, which is shorter than its diff:
```python
import functools
import math

import jax
import jax.numpy as jnp
from jax import lax
from jax.experimental import pallas as pl
from jax.experimental.pallas import tpu as pltpu
from jax.sharding import PartitionSpec as P

F32 = jnp.float32
BF16 = jnp.bfloat16
MESH = pl.DeviceIdType.MESH
CHUNKS = 2
ONE_X = 64
ONE_Z = 67
LEFT = 96


def split3(v):
    a = v.astype(BF16).astype(F32)
    b = (v - a).astype(BF16).astype(F32)
    return a, b, v - a - b


def packed(scaled, extra, first_sq, first_one):
    rows = scaled.shape[0]
    a, b, c = split3(-0.5 * jnp.sum(scaled * scaled, axis=1, keepdims=True))
    lane = lax.broadcasted_iota(jnp.int32, (rows, 128), 1)
    out = jnp.concatenate([scaled, extra], axis=1)
    out = jnp.where((lane >= first_one) & (lane < first_one + 3), 1.0, out)
    out = jnp.where(lane == first_sq, a, out)
    out = jnp.where(lane == first_sq + 1, b, out)
    return jnp.where(lane == first_sq + 2, c, out)


def kernel(
    n, nrow, total, feat_ref, left_ref, pts_ref, right_ref, inv_ref, slab_ref, point_ref,
    pk, pkt, zp, zpt, rpt, gz, tr, back_out, back_in, a_own, a_in, b_own, b_in,
    g_send, g_recv, r_send, r_recv, a_send, a_recv, b_send, b_recv,
):
    me = lax.axis_index("col")
    row = lax.axis_index("row")
    core = row % 2
    mate = row + 1 - 2 * core
    across = ((row // 2 + 1) % 2) * 2
    rows, width = feat_ref.shape
    ranks = left_ref.shape[1]
    chunks, _, cols = zpt.shape
    half = rows // 2

    def peer(d):
        out = 0
        bit = 1
        while bit < n:
            out = out + (((me // bit) % 2 + (d // bit) % 2) % 2) * bit
            bit *= 2
        return out

    barrier = pltpu.get_barrier_semaphore()
    for d in range(1, n):
        pl.semaphore_signal(barrier, inc=1, device_id={"col": peer(d)}, device_id_type=MESH)
    for r in (mate, across, across + 1):
        pl.semaphore_signal(barrier, inc=1, device_id={"row": r}, device_id_type=MESH)

    inv = inv_ref[...]
    xs = (feat_ref[...].astype(F32) * inv).astype(BF16).astype(F32)
    rank = lax.broadcasted_iota(jnp.int32, (rows, ranks), 1)
    coef = jnp.where(rank == 0, jnp.float32(0.5), jnp.float32(-0.5 / (ranks - 1)))
    left = left_ref[...].astype(F32) * coef * (64.0 / math.sqrt(total))
    extra = jnp.concatenate([jnp.zeros((rows, LEFT - width), F32), left], axis=1)
    pk[0] = packed(xs, extra, ONE_Z, ONE_X).astype(BF16)
    pl.semaphore_wait(barrier, n + 2)

    def gather(d):
        return pltpu.make_async_remote_copy(
            src_ref=pk.at[0], dst_ref=pk.at[d], send_sem=g_send.at[d], recv_sem=g_recv.at[d],
            device_id={"col": peer(d)}, device_id_type=MESH,
        )

    def giveback(d):
        return pltpu.make_async_remote_copy(
            src_ref=back_out.at[d], dst_ref=back_in.at[d], send_sem=r_send.at[d],
            recv_sem=r_recv.at[d], device_id={"col": peer(d)}, device_id_type=MESH,
        )

    def stage_a(h):
        return pltpu.make_async_remote_copy(
            src_ref=a_own.at[h], dst_ref=a_in.at[h], send_sem=a_send.at[h],
            recv_sem=a_recv.at[h], device_id={"row": mate}, device_id_type=MESH,
        )

    def stage_b(h, side, slot):
        return pltpu.make_async_remote_copy(
            src_ref=b_own.at[h, slot], dst_ref=b_in.at[h, slot], send_sem=b_send.at[h, side],
            recv_sem=b_recv.at[h, slot], device_id={"row": across + side}, device_id_type=MESH,
        )

    for d in range(1, n):
        gather(d).start()

    for h in range(chunks):
        part = pl.ds(h * cols, cols)
        zs = (pts_ref[part, :].astype(F32) * inv).astype(BF16).astype(F32)
        zpk = packed(zs, jnp.zeros((cols, 128 - width), F32), ONE_X, ONE_Z)
        zp[h] = zpk.astype(BF16)
        zpt[h] = zpk.T.astype(BF16)
        rp = jnp.concatenate(
            [jnp.zeros((cols, LEFT), F32), right_ref[part, :].astype(F32)], axis=1
        )
        rpt[h] = rp.T.astype(BF16)

    def send_a(h):
        zt = zpt[h, :width, :].astype(F32)
        term = tr[:width, :] - tr[ONE_X:ONE_X + 1, :] * zt
        a_own[h] = term.astype(BF16)
        stage_a(h).start()

    def send_b(h):
        stage_a(h).wait()
        s = (a_own[h].astype(F32) + a_in[h].astype(F32)).astype(BF16)
        b_own[h, 0] = s[:, : cols // 2]
        b_own[h, 1] = s[:, cols // 2:]
        for side in range(2):
            stage_b(h, side, core).start()

    def finish(h):
        for side in range(2):
            stage_b(h, side, core).wait_send()
        for slot in range(2):
            stage_b(h, 0, slot).wait_recv()
        for slot in range(2):
            tot = b_own[h, slot].astype(F32) + b_in[h, slot].astype(F32)
            w = cols // 2
            point_ref[pl.ds(h * cols + slot * w, w), :] = tot.T * inv

    def step(i, carry):
        h = i // n
        k = i % n
        last = h == chunks - 1
        d = jnp.where(last, n - 1 - k, k)

        @pl.when((h == 0) & (d > 0))
        def _():
            gather(d).wait()

        @pl.when(h == 0)
        def _():
            pkt[d] = pk[d].astype(F32).T[: pkt.shape[1], :].astype(BF16)

        block = pk[d]
        arg = jnp.dot(block, zpt[h], preferred_element_type=F32)
        weight = jnp.dot(block, rpt[h], preferred_element_type=F32)
        prod = (weight * jnp.exp(arg)).astype(BF16)
        g = jnp.dot(prod, zp[h], preferred_element_type=F32)
        t = jnp.dot(pkt[d], prod, preferred_element_type=F32)
        gz[d] = jnp.where(h == 0, 0.0, gz[d]) + g
        tr[...] = jnp.where(k == 0, 0.0, tr[...]) + t

        @pl.when(last)
        def _():
            acc = gz[d]
            term = acc[:, :width] - acc[:, ONE_Z:ONE_Z + 1] * pk[d][:, :width].astype(F32)
            both = jnp.concatenate([term[:half], term[half:]], axis=1)

            @pl.when(d > 0)
            def _():
                back_out[d] = both.astype(BF16)
                giveback(d).start()

            @pl.when(d == 0)
            def _():
                gz[0] = jnp.concatenate([both, both], axis=0)

        @pl.when(k == n - 1)
        def _():
            send_a(h)

        @pl.when((h > 0) & (k == 1))
        def _():
            send_b(h - 1)

        @pl.when((h > 0) & (k == n - 2))
        def _():
            finish(h - 1)

        return carry

    lax.fori_loop(0, chunks * n, step, 0)

    for d in range(1, n):
        giveback(d).wait()

    def add(d, acc):
        return acc + back_in[d].astype(F32)

    acc = lax.fori_loop(1, n, add, gz[0, :half, :])
    slab_ref[:half, :] = acc[:, :width] * inv
    slab_ref[half:, :] = acc[:, width:] * inv
    send_b(chunks - 1)
    finish(chunks - 1)


def local(n, nrow, slab_feat, slab_left, points, right_vec, inv_length):
    rows, width = slab_feat.shape
    npts = points.shape[0]
    cols = npts // CHUNKS
    vm = pl.BlockSpec(memory_space=pltpu.VMEM)
    dma = pltpu.SemaphoreType.DMA
    flops = 2 * n * rows * npts * 4 * 128
    return pl.pallas_call(
        functools.partial(kernel, n, nrow, npts * n),
        out_shape=(
            jax.ShapeDtypeStruct((rows, width), F32),
            jax.ShapeDtypeStruct((npts, width), F32),
        ),
        in_specs=[vm] * 5,
        out_specs=(vm, vm),
        scratch_shapes=[
            pltpu.VMEM((n, rows, 128), BF16),
            pltpu.VMEM((n, 80, rows), BF16),
            pltpu.VMEM((CHUNKS, cols, 128), BF16),
            pltpu.VMEM((CHUNKS, 128, cols), BF16),
            pltpu.VMEM((CHUNKS, 128, cols), BF16),
            pltpu.VMEM((n, rows, 128), F32),
            pltpu.VMEM((80, cols), F32),
            pltpu.VMEM((n, rows // 2, 128), BF16),
            pltpu.VMEM((n, rows // 2, 128), BF16),
            pltpu.VMEM((CHUNKS, width, cols), BF16),
            pltpu.VMEM((CHUNKS, width, cols), BF16),
            pltpu.VMEM((CHUNKS, 2, width, cols // 2), BF16),
            pltpu.VMEM((CHUNKS, 2, width, cols // 2), BF16),
            dma((n,)),
            dma((n,)),
            dma((n,)),
            dma((n,)),
            dma((CHUNKS,)),
            dma((CHUNKS,)),
            dma((CHUNKS, 2)),
            dma((CHUNKS, 2)),
        ],
        compiler_params=pltpu.CompilerParams(
            collective_id=0, has_side_effects=True, vmem_limit_bytes=48 * 1024 * 1024
        ),
        cost_estimate=pl.CostEstimate(
            flops=flops, bytes_accessed=4 * 1024 * 1024, transcendentals=n * rows * npts
        ),
    )(slab_feat, slab_left, points, right_vec, inv_length.reshape(1, width))


def solution(mesh):
    placed = (P(("row", "col"), None), P(("row", "col"), None), P("col", None), P("col", None), P())
    return jax.shard_map(
        functools.partial(local, mesh.shape["col"], mesh.shape["row"]),
        mesh=mesh,
        in_specs=placed,
        out_specs=(P(("row", "col"), None), P("col", None)),
        check_vma=False,
    )
```

time: 213 us -> 38.4 us (0.18); the launches traced: 209 us -> 38.2 us
  waiting for transfers between devices: 78.1 us -> 0 us
  blocking collectives: 50.3 us -> 0 us
  matrix products: 35.7 us -> 0 us
  Pallas kernels: 0 us -> 32.8 us
  local copies, waits for them, and re-layouts: 25.7 us -> 4.73 us
  between operations: 15.6 us -> 0.69 us
  other arithmetic: 3.41 us -> 0 us
    all_gather x2 -> x0, blocking collectives: 50.3 us -> none  [the longest x1 25.9 us: local(): lax.all_gather(xs, 'col', axis=0, tiled=True)]
    psum x1 -> x0, waiting for transfers between devices: 44.7 us -> none  [local(): point_grad = lax.psum(col_term, 'row')]
    dot_general x32 -> x0, matrix products: 35.7 us -> none  [the longest x8 11.4 us: col_step(): jnp.einsum('ik,jk->ij', x_blk, z_blk, preferred_element_type=jnp.float32)]
    reduce_scatter x1 -> x0, waiting for transfers between devices: 32.8 us -> none  [local(): lax.psum_scatter(row_term, 'col', scatter_dimension=0, tiled=True)]
    pallas_call x0 -> x1, Pallas kernels: none -> 32.8 us  [local(): pl.pallas_call(functools.partial(kernel, n, nrow, npts * n), out_shape=(j...]
    dynamic_update_slice x24 -> x0, local copies, waits for them, and re-layouts: 20 us -> none  [row_step(): lax.scan(col_step, start, (zs_blocks, right_blocks, sqz_blocks))]
    unnamed x13 -> x10, local copies, waits for them, and re-layouts: 5.66 us -> 2.91 us
  transfers between devices with their start and end apart: 2 -> 0, of which waited for: 2 -> 0; matrix products, arithmetic and copies ran while one was open for 0% -> 0% of each run, Pallas kernels for 0% -> 0%
where the time goes in v1:
time: 38.4 us; the launch traced here: 38.2 us
  Pallas kernels  32.8 us (85%)
  local copies, waits for them, and re-layouts  4.73 us (12%)
  between operations  0.69 us (2%)
    pallas_call x1, Pallas kernels, local(): pl.pallas_call(functools.partial(kernel, n, nrow, npts * n), out_shape=(j...  32.8 us
    unnamed x10, local copies, waits for them, and re-layouts  2.91 us
    pallas_call x2, local copies, waits for them, and re-layouts, local(): pl.pallas_call(functools.partial(kernel, n, nrow, npts * n), out_shape=(j...  1.83 us

profile of v1, /device:TPU:1, one launch (start us, length us, event | category | flops | bytes accessed | tf_op | source)
XLA Modules:
  0.0 38.2 jit_solution(14839538011441419822)
XLA Ops:
  0.6 0.0 copy-start.2
  0.6 0.9 %copy.7.feat_ref = bf16[256,64]{1,0:T(8,128)(2,1)S(1)} copy(bf16[256,64]{0,1:T(8,128)(2,1)} %param.5) | data formatting | bytes 65536 | tf_op args[0]
  1.5 0.0 copy-done.2
  1.5 0.1 copy.8.left_ref
  1.6 0.0 copy-start.1
  1.7 1.3 %copy.9.pts_ref = bf16[2048,64]{1,0:T(8,128)(2,1)S(1)} copy(bf16[2048,64]{0,1:T(8,128)(2,1)} %param.7) | data formatting | bytes 524288 | tf_op args[2]
  2.9 0.0 copy-done.1
  2.9 0.0 copy-start
  2.9 0.3 copy.10.right_ref
  3.2 0.4 copy-done
  3.6 32.8 %shard_map.68 = (f32[256,64]{1,0:T(8,128)S(1)}, f32[2048,64]{1,0:T(8,128)S(1)}) custom-call(bf16[256,64]{1,0:T(8,128)(2,1)S(1)} %copy.7.feat_ref, bf16[256,32]{1,0:T(8,128)(2,1)S(1)} %copy.8.left_ref, bf16[2048,64]{1,0:T(8,128)(2,1)S(1)} %copy.9.pts_ref, bf16[2048,32]{1,0:T(8,128)(2,1)S(1)} %copy.10.right_ref, f32[1,64]{1,0:T(1,128)S(1)} %bitcast.1), custom_call_target="tpu_custom_call" | custom-call | flops 4294967296 | bytes 4194304 | tf_op jit(solution)/shard_map/pallas_call | solution.py:211
  36.4 0.7 %copy.11 = f32[256,64]{0,1:T(8,128)} copy(f32[256,64]{1,0:T(8,128)S(1)} %get-tuple-element.2) | data formatting | bytes 131072 | tf_op jit(solution)/shard_map/pallas_call | solution.py:211
  37.1 1.1 %copy.12 = f32[2048,64]{0,1:T(8,128)} copy(f32[2048,64]{1,0:T(8,128)S(1)} %get-tuple-element.3) | data formatting | bytes 1048576 | tf_op jit(solution)/shard_map/pallas_call | solution.py:211
Async XLA Ops:
  0.6 0.9 %copy-start.2 = (bf16[256,32]{0,1:T(8,128)(2,1)S(1)}, bf16[256,32]{0,1:T(8,128)(2,1)}, u32[]{:S(2)}) copy-start(bf16[256,32]{0,1:T(8,128)(2,1)} %param.6) | copy-start | bytes 49156
  1.6 1.3 %copy-start.1 = (bf16[2048,32]{0,1:T(8,128)(2,1)S(1)}, bf16[2048,32]{0,1:T(8,128)(2,1)}, u32[]{:S(2)}) copy-start(bf16[2048,32]{0,1:T(8,128)(2,1)} %param.8) | copy-start | bytes 393220
  2.9 0.7 %copy-start = (f32[64]{0:T(128)S(1)}, f32[64]{0:T(128)}, u32[]{:S(2)}) copy-start(f32[64]{0:T(128)} %param.9) | copy-start | bytes 772

commit v2 on v1

v2 whole, which is shorter than its diff:
```python
import functools
import math

import jax
import jax.numpy as jnp
from jax import lax
from jax.experimental import pallas as pl
from jax.experimental.pallas import tpu as pltpu
from jax.sharding import PartitionSpec as P

F32 = jnp.float32
BF16 = jnp.bfloat16
MESH = pl.DeviceIdType.MESH
CHUNKS = 2
ONE_X = 64
ONE_Z = 67
LEFT = 80


def split3(v):
    a = v.astype(BF16).astype(F32)
    b = (v - a).astype(BF16).astype(F32)
    return a, b, v - a - b


def tail_rows(scaled, first_sq, first_one):
    a, b, c = split3(-0.5 * jnp.sum(scaled * scaled, axis=0, keepdims=True))
    line = lax.broadcasted_iota(jnp.int32, (16, scaled.shape[1]), 0) + 64
    out = jnp.where((line >= first_one) & (line < first_one + 3), 1.0, 0.0)
    out = jnp.where(line == first_sq, a, out)
    out = jnp.where(line == first_sq + 1, b, out)
    return jnp.where(line == first_sq + 2, c, out)


def kernel(
    n, total, feat_hbm, left_hbm, pts_hbm, right_hbm, inv_hbm, slab_ref, point_ref,
    feat_ref, left_ref, pts_ref, right_ref, inv_ref,
    gin, pk, pkt, zp, zpt, rpt, gz, tr, back_out, back_in, a_own, a_in, b_own, b_in,
    l_sem, g_send, g_recv, f_send, r_send, r_recv, a_send, a_recv, b_send, b_recv,
):
    me = lax.axis_index("col")
    row = lax.axis_index("row")
    core = row % 2
    mate = row + 1 - 2 * core
    across = ((row // 2 + 1) % 2) * 2
    width, rows = feat_ref.shape
    ranks = left_ref.shape[0]
    chunks, _, cols = zpt.shape

    loads = [
        pltpu.make_async_copy(src, dst, l_sem.at[i])
        for i, (src, dst) in enumerate((
            (inv_hbm, inv_ref), (feat_hbm, feat_ref), (left_hbm, left_ref),
            (pts_hbm, pts_ref), (right_hbm, right_ref),
        ))
    ]
    for load in loads:
        load.start()

    def peer(d):
        out = 0
        bit = 1
        while bit < n:
            out = out + (((me // bit) % 2 + (d // bit) % 2) % 2) * bit
            bit *= 2
        return out

    barrier = pltpu.get_barrier_semaphore()
    for d in range(1, n):
        pl.semaphore_signal(barrier, inc=1, device_id={"col": peer(d)}, device_id_type=MESH)
    for r in (mate, across, across + 1):
        pl.semaphore_signal(barrier, inc=1, device_id={"row": r}, device_id_type=MESH)

    loads[0].wait()
    eye = lax.broadcasted_iota(jnp.int32, (width, width), 0) == lax.broadcasted_iota(
        jnp.int32, (width, width), 1
    )
    inv = jnp.sum(jnp.where(eye, inv_ref[...], 0.0), axis=1, keepdims=True)
    loads[1].wait()
    loads[2].wait()
    gin[0, :width, :] = (feat_ref[...].astype(F32) * inv).astype(BF16)
    rank = lax.broadcasted_iota(jnp.int32, (ranks, rows), 0)
    coef = jnp.where(rank == 0, jnp.float32(0.5), jnp.float32(-0.5 / (ranks - 1)))
    gin[0, width:, :] = (left_ref[...].astype(F32) * coef * (64.0 / math.sqrt(total))).astype(BF16)
    pl.semaphore_wait(barrier, n + 2)

    def gather(d):
        return pltpu.make_async_remote_copy(
            src_ref=gin.at[0], dst_ref=gin.at[d], send_sem=g_send.at[d], recv_sem=g_recv.at[d],
            device_id={"col": peer(d)}, device_id_type=MESH,
        )

    def forward(d):
        return pltpu.make_async_remote_copy(
            src_ref=gin.at[d], dst_ref=gin.at[d + 1], send_sem=f_send.at[d],
            recv_sem=g_recv.at[d + 1], device_id={"col": peer(1)}, device_id_type=MESH,
        )

    def giveback(d):
        return pltpu.make_async_remote_copy(
            src_ref=back_out.at[d], dst_ref=back_in.at[d], send_sem=r_send.at[d],
            recv_sem=r_recv.at[d], device_id={"col": peer(d)}, device_id_type=MESH,
        )

    def stage_a(h):
        return pltpu.make_async_remote_copy(
            src_ref=a_own.at[h], dst_ref=a_in.at[h], send_sem=a_send.at[h],
            recv_sem=a_recv.at[h], device_id={"row": mate}, device_id_type=MESH,
        )

    def stage_b(h, side, slot):
        return pltpu.make_async_remote_copy(
            src_ref=b_own.at[h, slot], dst_ref=b_in.at[h, slot], send_sem=b_send.at[h, side],
            recv_sem=b_recv.at[h, slot], device_id={"row": across + side}, device_id_type=MESH,
        )

    for d in range(2, n, 2):
        gather(d).start()
    gather(1).start()

    loads[3].wait()
    loads[4].wait()
    for h in range(chunks):
        part = pl.ds(h * cols, cols)
        zs = (pts_ref[:, part].astype(F32) * inv).astype(BF16).astype(F32)
        zt = jnp.concatenate(
            [zs, tail_rows(zs, ONE_X, ONE_Z), jnp.zeros((128 - LEFT, cols), F32)], axis=0
        )
        zpt[h] = zt.astype(BF16)
        zp[h] = zt.T.astype(BF16)
        rpt[h] = jnp.concatenate(
            [
                jnp.zeros((LEFT, cols), BF16),
                right_ref[:, part],
                jnp.zeros((128 - LEFT - ranks, cols), BF16),
            ],
            axis=0,
        )

    def send_a(h):
        zt = zpt[h, :width, :].astype(F32)
        term = tr[:width, :] - tr[ONE_X:ONE_X + 1, :] * zt
        a_own[h] = term.astype(BF16)
        stage_a(h).start()

    def send_b(h):
        stage_a(h).wait()
        s = (a_own[h].astype(F32) + a_in[h].astype(F32)).astype(BF16)
        b_own[h, 0] = s[:, : cols // 2]
        b_own[h, 1] = s[:, cols // 2:]
        for side in range(2):
            stage_b(h, side, core).start()

    def finish(h):
        for side in range(2):
            stage_b(h, side, core).wait_send()
        for slot in range(2):
            stage_b(h, 0, slot).wait_recv()
        w = cols // 2
        for slot in range(2):
            tot = b_own[h, slot].astype(F32) + b_in[h, slot].astype(F32)
            point_ref[:, pl.ds(pl.multiple_of(h * cols + slot * w, w), w)] = tot * inv

    def step(i, carry):
        h = i // n
        k = i % n
        last = h == chunks - 1
        even = k <= n // 2
        near = jnp.where(k < 2, k, jnp.where(even, 2 * k - 2, 2 * k - n + 1))
        d = jnp.where(last, n - 1 - k, near)

        @pl.when((h == 0) & (k > 0))
        def _():
            gather(d).wait_recv()

        @pl.when((h == 0) & (k > 1) & even)
        def _():
            forward(d).start()

        @pl.when(h == 0)
        def _():
            x = gin[d].astype(F32)
            xs = x[:width]
            both = jnp.concatenate(
                [
                    xs, tail_rows(xs, ONE_Z, ONE_X), x[width:],
                    jnp.zeros((128 - LEFT - ranks, rows), F32),
                ],
                axis=0,
            )
            pkt[d] = both[:LEFT].astype(BF16)
            pk[d] = both.T.astype(BF16)

        block = pk[d]
        arg = jnp.dot(block, zpt[h], preferred_element_type=F32)
        weight = jnp.dot(block, rpt[h], preferred_element_type=F32)
        prod = (weight * jnp.exp(arg)).astype(BF16)
        g = jnp.dot(prod, zp[h], preferred_element_type=F32)
        t = jnp.dot(pkt[d], prod, preferred_element_type=F32)
        gz[d] = jnp.where(h == 0, 0.0, gz[d]) + g
        tr[...] = jnp.where(k == 0, 0.0, tr[...]) + t

        @pl.when(last)
        def _():
            acc = gz[d].T
            term = acc[:width] - acc[ONE_Z:ONE_Z + 1] * pkt[d][:width].astype(F32)

            @pl.when(d > 0)
            def _():
                back_out[d] = term.astype(BF16)
                giveback(d).start()

            @pl.when(d == 0)
            def _():
                slab_ref[...] = term

        @pl.when(k == n - 1)
        def _():
            send_a(h)

        @pl.when((h > 0) & (k == 1))
        def _():
            send_b(h - 1)

        @pl.when((h > 0) & (k == n - 2))
        def _():
            finish(h - 1)

        return carry

    lax.fori_loop(0, chunks * n, step, 0)

    gather(1).wait_send()
    for d in range(2, n, 2):
        gather(d).wait_send()
        forward(d).wait_send()
    for d in range(1, n):
        giveback(d).wait()

    def add(d, acc):
        return acc + back_in[d].astype(F32)

    acc = lax.fori_loop(1, n, add, slab_ref[...])
    slab_ref[...] = acc * inv
    send_b(chunks - 1)
    finish(chunks - 1)


def local(n, slab_feat, slab_left, points, right_vec, inv_length):
    rows, width = slab_feat.shape
    ranks = slab_left.shape[1]
    npts = points.shape[0]
    cols = npts // CHUNKS
    vm = pl.BlockSpec(memory_space=pltpu.VMEM)
    hbm = pl.BlockSpec(memory_space=pl.ANY)
    dma = pltpu.SemaphoreType.DMA
    flops = 2 * n * rows * npts * 4 * 128
    slab, point = pl.pallas_call(
        functools.partial(kernel, n, npts * n),
        out_shape=(
            jax.ShapeDtypeStruct((width, rows), F32),
            jax.ShapeDtypeStruct((width, npts), F32),
        ),
        in_specs=[hbm] * 5,
        out_specs=(vm, vm),
        scratch_shapes=[
            pltpu.VMEM((width, rows), BF16),
            pltpu.VMEM((ranks, rows), BF16),
            pltpu.VMEM((width, npts), BF16),
            pltpu.VMEM((ranks, npts), BF16),
            pltpu.VMEM((1, width), F32),
            pltpu.VMEM((n, width + ranks, rows), BF16),
            pltpu.VMEM((n, rows, 128), BF16),
            pltpu.VMEM((n, LEFT, rows), BF16),
            pltpu.VMEM((CHUNKS, cols, 128), BF16),
            pltpu.VMEM((CHUNKS, 128, cols), BF16),
            pltpu.VMEM((CHUNKS, 128, cols), BF16),
            pltpu.VMEM((n, rows, 128), F32),
            pltpu.VMEM((LEFT, cols), F32),
            pltpu.VMEM((n, width, rows), BF16),
            pltpu.VMEM((n, width, rows), BF16),
            pltpu.VMEM((CHUNKS, width, cols), BF16),
            pltpu.VMEM((CHUNKS, width, cols), BF16),
            pltpu.VMEM((CHUNKS, 2, width, cols // 2), BF16),
            pltpu.VMEM((CHUNKS, 2, width, cols // 2), BF16),
            dma((5,)),
            dma((n,)),
            dma((n,)),
            dma((n,)),
            dma((n,)),
            dma((n,)),
            dma((CHUNKS,)),
            dma((CHUNKS,)),
            dma((CHUNKS, 2)),
            dma((CHUNKS, 2)),
        ],
        compiler_params=pltpu.CompilerParams(
            collective_id=0, has_side_effects=True, vmem_limit_bytes=48 * 1024 * 1024
        ),
        cost_estimate=pl.CostEstimate(
            flops=flops, bytes_accessed=4 * 1024 * 1024, transcendentals=n * rows * npts
        ),
    )(slab_feat.T, slab_left.T, points.T, right_vec.T, inv_length.reshape(1, width))
    return slab.T, point.T


def solution(mesh):
    placed = (P(("row", "col"), None), P(("row", "col"), None), P("col", None), P("col", None), P())
    return jax.shard_map(
        functools.partial(local, mesh.shape["col"]),
        mesh=mesh,
        in_specs=placed,
        out_specs=(P(("row", "col"), None), P("col", None)),
        check_vma=False,
    )
```

time: 38.4 us -> 35 us (0.911)
  Pallas kernels: 32.8 us -> 28.6 us
  local copies, waits for them, and re-layouts: 4.73 us -> 5.4 us
    pallas_call x1, Pallas kernels: 32.8 us -> 28.6 us  [local(): pl.pallas_call(functools.partial(kernel, n, npts * n), out_shape=(jax.Sha...]
    unnamed x10 -> x12, local copies, waits for them, and re-layouts: 2.91 us -> 5.4 us
    pallas_call x2 -> x0, local copies, waits for them, and re-layouts: 1.83 us -> none  [local(): pl.pallas_call(functools.partial(kernel, n, nrow, npts * n), out_shape=(j...]
where the time goes in v2:
time: 35 us; the launch traced here: 34.7 us
  Pallas kernels  28.6 us (82%)
  local copies, waits for them, and re-layouts  5.4 us (15%)
  between operations  0.65 us (2%)
    pallas_call x1, Pallas kernels, local(): pl.pallas_call(functools.partial(kernel, n, npts * n), out_shape=(jax.Sha...  28.6 us
    unnamed x12, local copies, waits for them, and re-layouts  5.4 us

profile of v2, /device:TPU:1, one launch (start us, length us, event | category | flops | bytes accessed | tf_op | source)
XLA Modules:
  0.0 34.7 jit_solution(15145421552372227977)
XLA Ops:
  0.6 0.0 copy-start.4
  0.6 0.6 %copy-done.4 = f32[64]{0:T(128)S(1)} copy-done((f32[64]{0:T(128)S(1)}, f32[64]{0:T(128)}, u32[]{:S(2)}) %copy-start.4) | copy-done | bytes 280
  1.3 0.0 copy-start
  1.3 0.9 %copy-done = bf16[2048,64]{0,1:T(8,128)(2,1)S(1)} copy-done((bf16[2048,64]{0,1:T(8,128)(2,1)S(1)}, bf16[2048,64]{0,1:T(8,128)(2,1)}, u32[]{:S(2)}) %copy-start) | copy-done | bytes 262168
  2.2 0.0 copy-start.1
  2.2 0.9 %copy-done.1 = bf16[2048,32]{0,1:T(8,128)(2,1)S(1)} copy-done((bf16[2048,32]{0,1:T(8,128)(2,1)S(1)}, bf16[2048,32]{0,1:T(8,128)(2,1)}, u32[]{:S(2)}) %copy-start.1) | copy-done | bytes 131096
  3.1 0.0 copy-start.2
  3.1 0.8 %copy-done.2 = bf16[256,64]{0,1:T(8,128)(2,1)S(1)} copy-done((bf16[256,64]{0,1:T(8,128)(2,1)S(1)}, bf16[256,64]{0,1:T(8,128)(2,1)}, u32[]{:S(2)}) %copy-start.2) | copy-done | bytes 32792
  3.9 0.0 copy-start.3
  3.9 0.7 %copy-done.3 = bf16[256,32]{0,1:T(8,128)(2,1)S(1)} copy-done((bf16[256,32]{0,1:T(8,128)(2,1)S(1)}, bf16[256,32]{0,1:T(8,128)(2,1)}, u32[]{:S(2)}) %copy-start.3) | copy-done | bytes 16408
  4.6 28.6 %shard_map.68 = (f32[64,256]{1,0:T(8,128)S(1)}, f32[64,2048]{1,0:T(8,128)S(1)}) custom-call(bf16[64,256]{1,0:T(8,128)(2,1)S(1)} %bitcast.11, bf16[32,256]{1,0:T(8,128)(2,1)S(1)} %bitcast.12, bf16[64,2048]{1,0:T(8,128)(2,1)S(1)} %bitcast.9, bf16[32,2048]{1,0:T(8,128)(2,1)S(1)} %bitcast.10, f32[1,64]{1,0:T(1,128)S(1)} %bitcast.13), custom_call_target="tpu_custom_call" | custom-call | flops 4294967296 | bytes 4194304 | tf_op jit(solution)/shard_map/pallas_call | solution.py:258
  33.2 0.6 %copy.9 = f32[256,64]{0,1:T(8,128)} copy(f32[256,64]{0,1:T(8,128)S(1)} %bitcast.8) | data formatting | bytes 131072
  33.9 0.8 %copy.10 = f32[2048,64]{0,1:T(8,128)} copy(f32[2048,64]{0,1:T(8,128)S(1)} %bitcast.7) | data formatting | bytes 1048576
Async XLA Ops:
  0.6 0.7 %copy-start.4 = (f32[64]{0:T(128)S(1)}, f32[64]{0:T(128)}, u32[]{:S(2)}) copy-start(f32[64]{0:T(128)} %param.9) | copy-start | bytes 772
  1.3 0.9 %copy-start = (bf16[2048,64]{0,1:T(8,128)(2,1)S(1)}, bf16[2048,64]{0,1:T(8,128)(2,1)}, u32[]{:S(2)}) copy-start(bf16[2048,64]{0,1:T(8,128)(2,1)} %param.7) | copy-start | bytes 786436
  2.2 0.9 %copy-start.1 = (bf16[2048,32]{0,1:T(8,128)(2,1)S(1)}, bf16[2048,32]{0,1:T(8,128)(2,1)}, u32[]{:S(2)}) copy-start(bf16[2048,32]{0,1:T(8,128)(2,1)} %param.8) | copy-start | bytes 393220
  3.1 0.8 %copy-start.2 = (bf16[256,64]{0,1:T(8,128)(2,1)S(1)}, bf16[256,64]{0,1:T(8,128)(2,1)}, u32[]{:S(2)}) copy-start(bf16[256,64]{0,1:T(8,128)(2,1)} %param.5) | copy-start | bytes 98308
  3.9 0.7 %copy-start.3 = (bf16[256,32]{0,1:T(8,128)(2,1)S(1)}, bf16[256,32]{0,1:T(8,128)(2,1)}, u32[]{:S(2)}) copy-start(bf16[256,32]{0,1:T(8,128)(2,1)} %param.6) | copy-start | bytes 49156

commit v3 on v2

--- a/solution.py
+++ b/solution.py
@@ -33,10 +33,10 @@
 
 
 def kernel(
-    n, total, feat_hbm, left_hbm, pts_hbm, right_hbm, inv_hbm, slab_ref, point_ref,
-    feat_ref, left_ref, pts_ref, right_ref, inv_ref,
+    n, total, feat_hbm, left_hbm, pts_hbm, right_hbm, inv_hbm, slab_hbm, point_hbm,
+    feat_ref, left_ref, pts_ref, right_ref, inv_ref, slab_ref, point_ref,
     gin, pk, pkt, zp, zpt, rpt, gz, tr, back_out, back_in, a_own, a_in, b_own, b_in,
-    l_sem, g_send, g_recv, f_send, r_send, r_recv, a_send, a_recv, b_send, b_recv,
+    l_sem, o_sem, g_send, g_recv, f_send, r_send, r_recv, a_send, a_recv, b_send, b_recv,
 ):
     me = lax.axis_index("col")
     row = lax.axis_index("row")
@@ -137,9 +137,13 @@
             axis=0,
         )
 
+    def store(h):
+        part = pl.ds(pl.multiple_of(h * cols, cols), cols)
+        return pltpu.make_async_copy(point_ref.at[h], point_hbm.at[:, part], o_sem.at[h])
+
     def send_a(h):
         zt = zpt[h, :width, :].astype(F32)
-        term = tr[:width, :] - tr[ONE_X:ONE_X + 1, :] * zt
+        term = tr[h, :width, :] - tr[h, ONE_X:ONE_X + 1, :] * zt
         a_own[h] = term.astype(BF16)
         stage_a(h).start()
 
@@ -156,24 +160,25 @@
             stage_b(h, side, core).wait_send()
         for slot in range(2):
             stage_b(h, 0, slot).wait_recv()
-        w = cols // 2
-        for slot in range(2):
-            tot = b_own[h, slot].astype(F32) + b_in[h, slot].astype(F32)
-            point_ref[:, pl.ds(pl.multiple_of(h * cols + slot * w, w), w)] = tot * inv
+        tot = b_own[h].astype(F32) + b_in[h].astype(F32)
+        point_ref[h] = jnp.concatenate([tot[0], tot[1]], axis=1) * inv
+        store(h).start()
 
     def step(i, carry):
-        h = i // n
-        k = i % n
-        last = h == chunks - 1
+        early = i < 4
+        late = i >= n + 2
+        h = jnp.where(early, i % 2, jnp.where(late, 1, 0))
+        k = i - 2
         even = k <= n // 2
-        near = jnp.where(k < 2, k, jnp.where(even, 2 * k - 2, 2 * k - n + 1))
-        d = jnp.where(last, n - 1 - k, near)
-
-        @pl.when((h == 0) & (k > 0))
+        near = jnp.where(even, 2 * k - 2, 2 * k - n + 1)
+        d = jnp.where(early, i // 2, jnp.where(late, 2 * n + 1 - i, near))
+        last = h == 1
+
+        @pl.when((h == 0) & (d > 0))
         def _():
             gather(d).wait_recv()
 
-        @pl.when((h == 0) & (k > 1) & even)
+        @pl.when((h == 0) & (d > 1) & even)
         def _():
             forward(d).start()
 
@@ -198,7 +203,7 @@
         g = jnp.dot(prod, zp[h], preferred_element_type=F32)
         t = jnp.dot(pkt[d], prod, preferred_element_type=F32)
         gz[d] = jnp.where(h == 0, 0.0, gz[d]) + g
-        tr[...] = jnp.where(k == 0, 0.0, tr[...]) + t
+        tr[h] = jnp.where(d == 0, 0.0, tr[h]) + t
 
         @pl.when(last)
         def _():
@@ -214,36 +219,41 @@
             def _():
                 slab_ref[...] = term
 
-        @pl.when(k == n - 1)
-        def _():
-            send_a(h)
-
-        @pl.when((h > 0) & (k == 1))
-        def _():
-            send_b(h - 1)
-
-        @pl.when((h > 0) & (k == n - 2))
-        def _():
-            finish(h - 1)
+        @pl.when(i == n + 1)
+        def _():
+            send_a(0)
+
+        @pl.when(i == n + 3)
+        def _():
+            send_b(0)
+
+        @pl.when(i == 2 * n - 1)
+        def _():
+            send_a(1)
+            finish(0)
 
         return carry
 
-    lax.fori_loop(0, chunks * n, step, 0)
+    lax.fori_loop(0, 2 * n, step, 0)
 
     gather(1).wait_send()
     for d in range(2, n, 2):
         gather(d).wait_send()
         forward(d).wait_send()
+    send_b(1)
     for d in range(1, n):
         giveback(d).wait()
 
     def add(d, acc):
         return acc + back_in[d].astype(F32)
 
-    acc = lax.fori_loop(1, n, add, slab_ref[...])
-    slab_ref[...] = acc * inv
-    send_b(chunks - 1)
-    finish(chunks - 1)
+    slab_ref[...] = lax.fori_loop(1, n, add, slab_ref[...]) * inv
+    slab_store = pltpu.make_async_copy(slab_ref, slab_hbm, o_sem.at[chunks])
+    slab_store.start()
+    finish(1)
+    slab_store.wait()
+    store(0).wait()
+    store(1).wait()
 
 
 def local(n, slab_feat, slab_left, points, right_vec, inv_length):
@@ -251,7 +261,6 @@
     ranks = slab_left.shape[1]
     npts = points.shape[0]
     cols = npts // CHUNKS
-    vm = pl.BlockSpec(memory_space=pltpu.VMEM)
     hbm = pl.BlockSpec(memory_space=pl.ANY)
     dma = pltpu.SemaphoreType.DMA
     flops = 2 * n * rows * npts * 4 * 128
@@ -262,13 +271,15 @@
             jax.ShapeDtypeStruct((width, npts), F32),
         ),
         in_specs=[hbm] * 5,
-        out_specs=(vm, vm),
+        out_specs=(hbm, hbm),
         scratch_shapes=[
             pltpu.VMEM((width, rows), BF16),
             pltpu.VMEM((ranks, rows), BF16),
             pltpu.VMEM((width, npts), BF16),
             pltpu.VMEM((ranks, npts), BF16),
             pltpu.VMEM((1, width), F32),
+            pltpu.VMEM((width, rows), F32),
+            pltpu.VMEM((CHUNKS, width, cols), F32),
             pltpu.VMEM((n, width + ranks, rows), BF16),
             pltpu.VMEM((n, rows, 128), BF16),
             pltpu.VMEM((n, LEFT, rows), BF16),
@@ -276,7 +287,7 @@
             pltpu.VMEM((CHUNKS, 128, cols), BF16),
             pltpu.VMEM((CHUNKS, 128, cols), BF16),
             pltpu.VMEM((n, rows, 128), F32),
-            pltpu.VMEM((LEFT, cols), F32),
+            pltpu.VMEM((CHUNKS, LEFT, cols), F32),
             pltpu.VMEM((n, width, rows), BF16),
             pltpu.VMEM((n, width, rows), BF16),
             pltpu.VMEM((CHUNKS, width, cols), BF16),
@@ -284,6 +295,7 @@
             pltpu.VMEM((CHUNKS, 2, width, cols // 2), BF16),
             pltpu.VMEM((CHUNKS, 2, width, cols // 2), BF16),
             dma((5,)),
+            dma((CHUNKS + 1,)),
             dma((n,)),
             dma((n,)),
             dma((n,)),
@@ -295,7 +307,7 @@
             dma((CHUNKS, 2)),
         ],
         compiler_params=pltpu.CompilerParams(
-            collective_id=0, has_side_effects=True, vmem_limit_bytes=48 * 1024 * 1024
+            collective_id=0, has_side_effects=True, vmem_limit_bytes=125 * 512 * 1024
         ),
         cost_estimate=pl.CostEstimate(
             flops=flops, bytes_accessed=4 * 1024 * 1024, transcendentals=n * rows * npts

time: 35 us -> 32.9 us (0.940)
  local copies, waits for them, and re-layouts: 5.4 us -> 3.34 us
    unnamed x12 -> x2, local copies, waits for them, and re-layouts: 5.4 us -> 3.34 us
where the time goes in v3:
time: 32.9 us; the launch traced here: 32.6 us
  Pallas kernels  28.6 us (87%)
  local copies, waits for them, and re-layouts  3.34 us (10%)
  between operations  0.64 us (2%)
    pallas_call x1, Pallas kernels, local(): pl.pallas_call(functools.partial(kernel, n, npts * n), out_shape=(jax.Sha...  28.6 us
    unnamed x2, local copies, waits for them, and re-layouts  3.34 us

profile of v3, /device:TPU:1, one launch (start us, length us, event | category | flops | bytes accessed | tf_op | source)
XLA Modules:
  0.0 32.6 jit_solution(13502763283950189345)
XLA Ops:
  0.6 28.6 %shard_map.68 = (f32[64,256]{1,0:T(8,128)}, f32[64,2048]{1,0:T(8,128)}) custom-call(bf16[64,256]{1,0:T(8,128)(2,1)} %bitcast.11, bf16[32,256]{1,0:T(8,128)(2,1)} %bitcast.12, bf16[64,2048]{1,0:T(8,128)(2,1)} %bitcast.9, bf16[32,2048]{1,0:T(8,128)(2,1)} %bitcast.10, f32[1,64]{1,0:T(1,128)} %bitcast.13), custom_call_target="tpu_custom_call" | custom-call | flops 4294967296 | bytes 4194304 | tf_op jit(solution)/shard_map/pallas_call | solution.py:267
  29.3 1.5 %copy.9 = f32[256,64]{0,1:T(8,128)} copy(f32[256,64]{0,1:T(8,128)} %bitcast.8) | data formatting | bytes 131072
  30.8 1.9 %copy.10 = f32[2048,64]{0,1:T(8,128)} copy(f32[2048,64]{0,1:T(8,128)} %bitcast.7) | data formatting | bytes 1048576

commit v4 on v3

--- a/solution.py
+++ b/solution.py
@@ -33,10 +33,10 @@
 
 
 def kernel(
-    n, total, feat_hbm, left_hbm, pts_hbm, right_hbm, inv_hbm, slab_hbm, point_hbm,
-    feat_ref, left_ref, pts_ref, right_ref, inv_ref, slab_ref, point_ref,
+    n, total, feat_hbm, left_hbm, pts_hbm, right_hbm, inv_hbm, slab_ref, point_ref,
+    feat_ref, left_ref, pts_ref, right_ref, inv_ref,
     gin, pk, pkt, zp, zpt, rpt, gz, tr, back_out, back_in, a_own, a_in, b_own, b_in,
-    l_sem, o_sem, g_send, g_recv, f_send, r_send, r_recv, a_send, a_recv, b_send, b_recv,
+    l_sem, g_send, g_recv, f_send, r_send, r_recv, a_send, a_recv, b_send, b_recv,
 ):
     me = lax.axis_index("col")
     row = lax.axis_index("row")
@@ -137,10 +137,6 @@
             axis=0,
         )
 
-    def store(h):
-        part = pl.ds(pl.multiple_of(h * cols, cols), cols)
-        return pltpu.make_async_copy(point_ref.at[h], point_hbm.at[:, part], o_sem.at[h])
-
     def send_a(h):
         zt = zpt[h, :width, :].astype(F32)
         term = tr[h, :width, :] - tr[h, ONE_X:ONE_X + 1, :] * zt
@@ -161,8 +157,8 @@
         for slot in range(2):
             stage_b(h, 0, slot).wait_recv()
         tot = b_own[h].astype(F32) + b_in[h].astype(F32)
-        point_ref[h] = jnp.concatenate([tot[0], tot[1]], axis=1) * inv
-        store(h).start()
+        part = pl.ds(h * cols, cols)
+        point_ref[:, part] = jnp.concatenate([tot[0], tot[1]], axis=1) * inv
 
     def step(i, carry):
         early = i < 4
@@ -248,12 +244,7 @@
         return acc + back_in[d].astype(F32)
 
     slab_ref[...] = lax.fori_loop(1, n, add, slab_ref[...]) * inv
-    slab_store = pltpu.make_async_copy(slab_ref, slab_hbm, o_sem.at[chunks])
-    slab_store.start()
     finish(1)
-    slab_store.wait()
-    store(0).wait()
-    store(1).wait()
 
 
 def local(n, slab_feat, slab_left, points, right_vec, inv_length):
@@ -261,9 +252,11 @@
     ranks = slab_left.shape[1]
     npts = points.shape[0]
     cols = npts // CHUNKS
-    hbm = pl.BlockSpec(memory_space=pl.ANY)
+    vm = pl.BlockSpec(memory_space=pltpu.VMEM)
+    hbm = pl.BlockSpec(memory_space=pltpu.HBM)
     dma = pltpu.SemaphoreType.DMA
     flops = 2 * n * rows * npts * 4 * 128
+    operands = (slab_feat.T, slab_left.T, points.T, right_vec.T, inv_length.reshape(1, width))
     slab, point = pl.pallas_call(
         functools.partial(kernel, n, npts * n),
         out_shape=(
@@ -271,15 +264,13 @@
             jax.ShapeDtypeStruct((width, npts), F32),
         ),
         in_specs=[hbm] * 5,
-        out_specs=(hbm, hbm),
+        out_specs=(vm, vm),
         scratch_shapes=[
             pltpu.VMEM((width, rows), BF16),
             pltpu.VMEM((ranks, rows), BF16),
             pltpu.VMEM((width, npts), BF16),
             pltpu.VMEM((ranks, npts), BF16),
             pltpu.VMEM((1, width), F32),
-            pltpu.VMEM((width, rows), F32),
-            pltpu.VMEM((CHUNKS, width, cols), F32),
             pltpu.VMEM((n, width + ranks, rows), BF16),
             pltpu.VMEM((n, rows, 128), BF16),
             pltpu.VMEM((n, LEFT, rows), BF16),
@@ -295,7 +286,6 @@
             pltpu.VMEM((CHUNKS, 2, width, cols // 2), BF16),
             pltpu.VMEM((CHUNKS, 2, width, cols // 2), BF16),
             dma((5,)),
-            dma((CHUNKS + 1,)),
             dma((n,)),
             dma((n,)),
             dma((n,)),
@@ -307,12 +297,12 @@
             dma((CHUNKS, 2)),
         ],
         compiler_params=pltpu.CompilerParams(
-            collective_id=0, has_side_effects=True, vmem_limit_bytes=125 * 512 * 1024
+            collective_id=0, has_side_effects=True, vmem_limit_bytes=48 * 1024 * 1024
         ),
         cost_estimate=pl.CostEstimate(
             flops=flops, bytes_accessed=4 * 1024 * 1024, transcendentals=n * rows * npts
         ),
-    )(slab_feat.T, slab_left.T, points.T, right_vec.T, inv_length.reshape(1, width))
+    )(*[pltpu.with_memory_space_constraint(v, pltpu.HBM) for v in operands])
     return slab.T, point.T
 
 

time: 32.9 us -> 30.1 us (0.915)
  local copies, waits for them, and re-layouts: 3.34 us -> 1.42 us
  Pallas kernels: 28.6 us -> 27.9 us
    unnamed x2, local copies, waits for them, and re-layouts: 3.34 us -> 1.42 us
    pallas_call x1, Pallas kernels: 28.6 us -> 27.9 us  [local(): pl.pallas_call(functools.partial(kernel, n, npts * n), out_shape=(jax.Sha...]
where the time goes in v4:
time: 30.1 us; the launch traced here: 30 us
  Pallas kernels  27.9 us (93%)
  local copies, waits for them, and re-layouts  1.42 us (5%)
  between operations  0.64 us (2%)
    pallas_call x1, Pallas kernels, local(): pl.pallas_call(functools.partial(kernel, n, npts * n), out_shape=(jax.Sha...  27.9 us
    unnamed x2, local copies, waits for them, and re-layouts  1.42 us

profile of v4, /device:TPU:1, one launch (start us, length us, event | category | flops | bytes accessed | tf_op | source)
XLA Modules:
  0.0 30.0 jit_solution(4236125485071356343)
XLA Ops:
  0.6 27.9 %shard_map.68 = (f32[64,256]{1,0:T(8,128)S(1)}, f32[64,2048]{1,0:T(8,128)S(1)}) custom-call(bf16[64,256]{1,0:T(8,128)(2,1)} %bitcast.11, bf16[32,256]{1,0:T(8,128)(2,1)} %bitcast.12, bf16[64,2048]{1,0:T(8,128)(2,1)} %bitcast.9, bf16[32,2048]{1,0:T(8,128)(2,1)} %bitcast.10, f32[1,64]{1,0:T(1,128)} %bitcast.13), custom_call_target="tpu_custom_call" | custom-call | flops 4294967296 | bytes 4194304 | tf_op jit(solution)/shard_map/pallas_call | solution.py:260
  28.5 0.6 %copy.9 = f32[256,64]{0,1:T(8,128)} copy(f32[256,64]{0,1:T(8,128)S(1)} %bitcast.8) | data formatting | bytes 131072
  29.2 0.8 %copy.10 = f32[2048,64]{0,1:T(8,128)} copy(f32[2048,64]{0,1:T(8,128)S(1)} %bitcast.7) | data formatting | bytes 1048576

commit v5 on v4

--- a/solution.py
+++ b/solution.py
@@ -170,13 +170,14 @@
         d = jnp.where(early, i // 2, jnp.where(late, 2 * n + 1 - i, near))
         last = h == 1
 
-        @pl.when((h == 0) & (d > 0))
+        @pl.when((h == 0) & (d % 2 == 1))
         def _():
             gather(d).wait_recv()
 
-        @pl.when((h == 0) & (d > 1) & even)
-        def _():
-            forward(d).start()
+        @pl.when((i >= 3) & (i < n // 2 + 2))
+        def _():
+            gather(2 * (i - 2)).wait_recv()
+            forward(2 * (i - 2)).start()
 
         @pl.when(h == 0)
         def _():

time: 30.1 us -> 29.2 us (0.970)
  Pallas kernels: 27.9 us -> 27 us
    pallas_call x1, Pallas kernels: 27.9 us -> 27 us  [local(): pl.pallas_call(functools.partial(kernel, n, npts * n), out_shape=(jax.Sha...]
where the time goes in v5:
time: 29.2 us; the launch traced here: 29.1 us
  Pallas kernels  27 us (92%)
  local copies, waits for them, and re-layouts  1.42 us (5%)
  between operations  0.64 us (2%)
    pallas_call x1, Pallas kernels, local(): pl.pallas_call(functools.partial(kernel, n, npts * n), out_shape=(jax.Sha...  27 us
    unnamed x2, local copies, waits for them, and re-layouts  1.42 us

profile of v5, /device:TPU:1, one launch (start us, length us, event | category | flops | bytes accessed | tf_op | source)
XLA Modules:
  0.0 29.1 jit_solution(1165512651385748256)
XLA Ops:
  0.6 27.0 %shard_map.68 = (f32[64,256]{1,0:T(8,128)S(1)}, f32[64,2048]{1,0:T(8,128)S(1)}) custom-call(bf16[64,256]{1,0:T(8,128)(2,1)} %bitcast.11, bf16[32,256]{1,0:T(8,128)(2,1)} %bitcast.12, bf16[64,2048]{1,0:T(8,128)(2,1)} %bitcast.9, bf16[32,2048]{1,0:T(8,128)(2,1)} %bitcast.10, f32[1,64]{1,0:T(1,128)} %bitcast.13), custom_call_target="tpu_custom_call" | custom-call | flops 4294967296 | bytes 4194304 | tf_op jit(solution)/shard_map/pallas_call | solution.py:261
  27.6 0.6 %copy.9 = f32[256,64]{0,1:T(8,128)} copy(f32[256,64]{0,1:T(8,128)S(1)} %bitcast.8) | data formatting | bytes 131072
  28.3 0.8 %copy.10 = f32[2048,64]{0,1:T(8,128)} copy(f32[2048,64]{0,1:T(8,128)S(1)} %bitcast.7) | data formatting | bytes 1048576
